TPU v7x, 512 devices: a whole 4x4x16 slice. The times are simulated.
512 devices in a mesh: dp: 16 (over x_lo, y, core), tensor: 32 (over z, x_hi).
Axes of the slice: x: 4 (x_hi: 2, x_lo: 2; x = x_hi * 2 + x_lo), y: 4, z: 16, core: 2. Of those that a mesh axis runs over, the one named last changes fastest.
Arguments:
- tokens: bfloat16 [2048, 8192], P(('dp', 'tensor')), may hold values from -6 to 6
- gate_weight: bfloat16 [8192, 28672], P('dp', 'tensor'), may hold values from -0.0625 to 0.0625
- up_weight: bfloat16 [8192, 28672], P('dp', 'tensor'), may hold values from -0.0625 to 0.0625
- hidden_grad: bfloat16 [2048, 28672], P('dp', 'tensor'), may hold values from -1.5 to 1.5
Outputs:
- hidden: bfloat16 [2048, 28672], P('dp', 'tensor')
- tokens_grad: bfloat16 [2048, 8192], P(('dp', 'tensor'))
- gate_grad: bfloat16 [8192, 28672], P('dp', 'tensor')
- up_grad: bfloat16 [8192, 28672], P('dp', 'tensor')
All inputs are finite; a program needn't handle non-finite values.
Results may differ from a plain program's by a relative error of at most 0.0049.
Values may be sent and summed in bfloat16 or wider, within the bound.
A program may use at most 128 MiB of HBM per device.

v0:
```python
import jax
import jax.numpy as jnp
from jax import lax
from jax.sharding import PartitionSpec as P


def per_device(tokens, gate_weight, up_weight, hidden_grad):
    groups = lax.axis_size("dp")
    rows = lax.all_gather(tokens, "tensor", axis=0, tiled=True)
    group_len = rows.shape[0]
    local_ff = gate_weight.shape[1]
    slices = lax.all_to_all(rows, "dp", split_axis=1, concat_axis=0, tiled=True)
    part_gate = jnp.dot(slices, gate_weight, preferred_element_type=jnp.float32)
    part_up = jnp.dot(slices, up_weight, preferred_element_type=jnp.float32)
    back_gate, back_up = (
        lax.all_to_all(part_gate, "dp", split_axis=0, concat_axis=1, tiled=True),
        lax.all_to_all(part_up, "dp", split_axis=0, concat_axis=1, tiled=True),
    )
    gate = jnp.sum(back_gate.reshape(group_len, groups, local_ff), axis=1)
    up = jnp.sum(back_up.reshape(group_len, groups, local_ff), axis=1)
    sig = jax.nn.sigmoid(gate)
    act = gate * sig
    hidden = (act * up).astype(jnp.bfloat16)
    cot = hidden_grad.astype(jnp.float32)
    gate_delta = (cot * up * sig * (1.0 + gate * (1.0 - sig))).astype(jnp.bfloat16)
    up_delta = (cot * act).astype(jnp.bfloat16)
    contract_rows = (((0,), (0,)), ((), ()))
    contract_cols = (((1,), (1,)), ((), ()))
    all_gate, all_up = (
        lax.all_gather(gate_delta, "dp", axis=0, tiled=True),
        lax.all_gather(up_delta, "dp", axis=0, tiled=True),
    )
    gate_grad = lax.dot_general(
        slices, all_gate, contract_rows, preferred_element_type=jnp.float32
    ).astype(jnp.bfloat16)
    up_grad = lax.dot_general(
        slices, all_up, contract_rows, preferred_element_type=jnp.float32
    ).astype(jnp.bfloat16)
    pieces = lax.dot_general(
        all_gate, gate_weight, contract_cols, preferred_element_type=jnp.float32
    )
    pieces = pieces + lax.dot_general(
        all_up, up_weight, contract_cols, preferred_element_type=jnp.float32
    )
    partial_value = lax.all_to_all(pieces, "dp", split_axis=0, concat_axis=1, tiled=True)
    tokens_grad = lax.psum_scatter(partial_value, "tensor", scatter_dimension=0, tiled=True).astype(
        jnp.bfloat16
    )
    return (hidden, tokens_grad, gate_grad, up_grad)


def solution(mesh):
    placed = (P(("dp", "tensor"), None), P("dp", "tensor"), P("dp", "tensor"), P("dp", "tensor"))
    return jax.shard_map(
        per_device,
        mesh=mesh,
        in_specs=placed,
        out_specs=(
            P("dp", "tensor"),
            P(("dp", "tensor"), None),
            P("dp", "tensor"),
            P("dp", "tensor"),
        ),
        check_vma=False,
    )
```

profile of v0, /device:TPU:8, one launch (start us, length us, event | category | flops | bytes accessed | tf_op | source)
XLA Modules:
  0.0 835.2 jit_solution(5904934854516145943)
XLA Ops:
  7.2 0.0 all-gather.9.cloned.1.call-start
  7.2 0.7 all-gather.9.cloned.1.call-update
  7.9 157.8 %all-gather.9.cloned.1.call-done = bf16[32,4,8192]{2,1,0:T(4,128)(2,1)} async-done(((bf16[1,4,8192]{2,1,0:T(4,128)(2,1)}), bf16[32,4,8192]{2,1,0:T(4,128)(2,1)}) %all-gather.9.cloned.1.call-update) | async-done | bytes 2097168 | tf_op jit(solution)/shard_map/all_gather | solution.py:9
  165.7 3.3 all_to_all.44
  169.0 1.2 copy.15
  170.2 28.9 %all_to_all.58 = bf16[128,16,512]{2,0,1:T(8,128)(2,1)S(1)} all-to-all(bf16[128,16,512]{2,0,1:T(8,128)(2,1)S(1)} %copy.15), channel_id=1, replica_groups=mesh['dp'=16,'tensor'=32] {'dp'}, dimensions={1} | all-to-all | bytes 4194304 | tf_op jit(solution)/shard_map/all_to_all | solution.py:12
  199.1 5.3 fusion
  204.4 7.9 all-to-all-start.2
  212.3 5.4 fusion.2
  217.7 103.9 %all-to-all-done.2 = f32[16,128,896]{2,1,0:T(8,128)} async-done(((f32[16,128,896]{2,1,0:T(8,128)}), f32[16,128,896]{2,1,0:T(8,128)}, u32[]{:S(2)}, u32[]{:S(2)}) %all-to-all-start.2) | async-done | bytes 7340064 | tf_op jit(solution)/shard_map/all_to_all | solution.py:17
  321.6 7.0 all-to-all-start.1
  328.6 0.0 all-gather.5.cloned.1.call-start
  328.6 3.5 reduce_sum.19
  332.1 106.4 %all-to-all-done.1 = f32[16,128,896]{2,1,0:T(8,128)} async-done(((f32[16,128,896]{2,1,0:T(8,128)}), f32[16,128,896]{2,1,0:T(8,128)}, u32[]{:S(2)}, u32[]{:S(2)}) %all-to-all-start.1) | async-done | bytes 7340064 | tf_op jit(solution)/shard_map/all_to_all | solution.py:16
  438.5 4.2 reduce_sum.18
  442.7 2.2 fusion.10
  445.0 0.0 all-gather.7.cloned.1.call-start
  445.0 0.7 all-gather.7.cloned.1.call-update
  445.7 39.7 %all-gather.5.cloned.1.call-done = bf16[2048,896]{1,0:T(8,128)(2,1)} async-done(((bf16[128,896]{1,0:T(8,128)(2,1)}), bf16[2048,896]{1,0:T(8,128)(2,1)}) %all-gather.5.cloned.1.call-update) | async-done | bytes 3670032 | tf_op jit(solution)/shard_map/all_gather | solution.py:30
  485.4 6.4 fusion.13
  491.8 40.3 %all-gather.7.cloned.1.call-done = bf16[2048,896]{1,0:T(8,128)(2,1)} async-done(((bf16[128,896]{1,0:T(8,128)(2,1)}), bf16[2048,896]{1,0:T(8,128)(2,1)}) %all-gather.7.cloned.1.call-update) | async-done | bytes 3670032 | tf_op jit(solution)/shard_map/all_gather | solution.py:31
  532.1 7.9 convolution_add_fusion
  540.0 5.4 all-to-all-start.3
  545.5 1.3 dynamic-slice
  547.4 5.0 fusion.4
  552.4 2.2 copy.17
  554.6 5.1 fusion.5
  559.7 2.2 copy.18
  561.9 42.2 %all-to-all-done.3 = f32[16,128,512]{2,1,0:T(8,128)} async-done(((f32[16,128,512]{2,1,0:T(8,128)}), f32[16,128,512]{2,1,0:T(8,128)}, u32[]{:S(2)}, u32[]{:S(2)}) %all-to-all-start.3) | async-done | bytes 4194336 | tf_op jit(solution)/shard_map/all_to_all | solution.py:45
  604.1 4.8 copy.19
  608.9 219.1 %all-reduce.2 = bf16[128,8192]{1,0:T(8,128)(2,1)S(1)} all-reduce(f32[128,8192]{1,0:T(8,128)} %bitcast.31), channel_id=2, replica_groups=mesh['dp'=16,'tensor'=32] {'tensor'}, use_global_device_ids=true, to_apply=%region_2.0.clone | all-reduce | flops 1048576 | bytes 6291456
  828.0 0.7 dynamic-slice_convert_fusion
  (5 shorter events, 0.0 us)
Async XLA Ops:
  7.2 205.2 %copy-start = (bf16[512,896]{1,0:T(8,128)(2,1)S(1)}, bf16[512,896]{1,0:T(8,128)(2,1)}, u32[]{:S(2)}) copy-start(bf16[512,896]{1,0:T(8,128)(2,1)} %param.5) | copy-start | bytes 2752516
  7.2 158.5 %all-gather.9.cloned.1.call-start = ((), (), s32[]{:S(2)}) async-start(), calls=%async_computation.6 | async-start | bytes 2162688 | tf_op jit(solution)/shard_map/all_gather | solution.py:9
  169.0 30.1 %copy-start.1 = (bf16[512,896]{1,0:T(8,128)(2,1)S(1)}, bf16[512,896]{1,0:T(8,128)(2,1)}, u32[]{:S(2)}) copy-start(bf16[512,896]{1,0:T(8,128)(2,1)} %param.6) | copy-start | bytes 2752516
  204.4 117.2 %all-to-all-start.2 = ((f32[16,128,896]{2,1,0:T(8,128)}), f32[16,128,896]{2,1,0:T(8,128)}, u32[]{:S(2)}, u32[]{:S(2)}) async-start(f32[16,128,896]{2,1,0:T(8,128)} %fusion), calls=%async_computation.2 | async-start | bytes 14680064 | tf_op jit(solution)/shard_map/all_to_all | solution.py:17
  321.6 116.9 %all-to-all-start.1 = ((f32[16,128,896]{2,1,0:T(8,128)}), f32[16,128,896]{2,1,0:T(8,128)}, u32[]{:S(2)}, u32[]{:S(2)}) async-start(f32[16,128,896]{2,1,0:T(8,128)} %fusion.2), calls=%async_computation.1 | async-start | bytes 14680064 | tf_op jit(solution)/shard_map/all_to_all | solution.py:16
  328.6 156.8 %all-gather.5.cloned.1.call-start = ((), (), s32[]{:S(2)}) async-start(), calls=%async_computation.4 | async-start | bytes 3899392 | tf_op jit(solution)/shard_map/all_gather | solution.py:30
  445.0 87.1 %all-gather.7.cloned.1.call-start = ((), (), s32[]{:S(2)}) async-start(), calls=%async_computation.5 | async-start | bytes 3899392 | tf_op jit(solution)/shard_map/all_gather | solution.py:31
  540.0 64.1 %all-to-all-start.3 = ((f32[16,128,512]{2,1,0:T(8,128)}), f32[16,128,512]{2,1,0:T(8,128)}, u32[]{:S(2)}, u32[]{:S(2)}) async-start(f32[16,128,512]{2,1,0:T(8,128)} %bitcast.32), calls=%async_computation.3 | async-start | bytes 8388608 | tf_op jit(solution)/shard_map/all_to_all | solution.py:45
Sparse Core Ops, SparseCore 0:
  11.1 154.5 all-gather.8
  445.1 40.2 all-gather.4
  487.5 44.5 all-gather.6
where the time goes:
time: 836 us; the launch traced here: 835 us
  waiting for transfers between devices  492 us (59%)
  blocking collectives  248 us (30%)
  matrix products  35.1 us (4%)
  starting transfers between devices  20.5 us (2%)
  local copies, waits for them, and re-layouts  15.6 us (2%)
  between operations  14.4 us (2%)
  other arithmetic  9.89 us (1%)
    unnamed x1, blocking collectives  219 us
    all_gather x1, waiting for transfers between devices, per_device(): rows = lax.all_gather(tokens, 'tensor', axis=0, tiled=True)  158 us
    all_to_all x1, waiting for transfers between devices, per_device(): lax.all_to_all(part_gate, 'dp', split_axis=0, concat_axis=1, tiled=True)  106 us
    all_to_all x1, waiting for transfers between devices, per_device(): lax.all_to_all(part_up, 'dp', split_axis=0, concat_axis=1, tiled=True)  104 us
    all_to_all x1, waiting for transfers between devices, per_device(): lax.all_to_all(pieces, 'dp', split_axis=0, concat_axis=1, tiled=True)  42.2 us
    all_gather x1, waiting for transfers between devices, per_device(): lax.all_gather(up_delta, 'dp', axis=0, tiled=True)  40.3 us
    all_gather x1, waiting for transfers between devices, per_device(): lax.all_gather(gate_delta, 'dp', axis=0, tiled=True)  39.7 us
    all_to_all x1, blocking collectives, per_device(): slices = lax.all_to_all(rows, 'dp', split_axis=1, concat_axis=0, tiled=True)  28.9 us
  transfers between devices with their start and end apart: 6, of which 6 were waited for; matrix products, arithmetic and copies ran while one was open for 4% of the time, Pallas kernels for 0%

commit v1 on v0

v1 whole, which is shorter than its diff:
```python
import functools

import jax
import jax.numpy as jnp
from jax import lax
from jax.experimental import pallas as pl
from jax.experimental.pallas import tpu as pltpu
from jax.sharding import PartitionSpec as P

MESH = pl.DeviceIdType.MESH
F32 = jnp.float32
BF16 = jnp.bfloat16
NZ = 16
NS = 8
CUT = 512
FIRST = 1
LOW = 3


def send(src, dst, send_sem, recv_sem, device):
    pltpu.make_async_remote_copy(
        src_ref=src,
        dst_ref=dst,
        send_sem=send_sem,
        recv_sem=recv_sem,
        device_id=device,
        device_id_type=MESH,
    ).start()


def take(ref, sem):
    pltpu.make_async_copy(ref, ref, sem).wait()


def kernel(
    tok_ref, gw_ref, uw_ref, hg_ref,
    hid_ref, tg_ref, gg_ref, ug_ref,
    wbuf, ts, ta, tb, asm, xbuf, xpt,
    sbuf, fbuf, gya, ux, gyb, gxs, gxr, gown, uacc, us, uya0, uya1, uyb,
    dbuf, pbuf, zacc, zs, zr, zsl, zrl,
    fs, fr, fown, ps, pr, ws, wr, wown,
    w_local, w_send, w_recv, t_send, t_recv, h_send, h_recv, az_send, az_recv,
    ssem, rsem, z_send, z_recv, zl_send, zl_recv, f_send, f_recv, p_send, p_recv, ww_send, ww_recv,
):
    dp, tensor = lax.axis_index("dp"), lax.axis_index("tensor")
    core = lax.rem(dp, 2)
    p = dp // 2
    y, xl = lax.rem(p, 4), p // 4
    xh, z = lax.rem(tensor, 2), tensor // 2
    yp, y2, ym = lax.rem(y + 1, 4), lax.rem(y + 2, 4), lax.rem(y + 3, 4)
    xo = 1 - xl

    def at(xx, yy):
        return ((xx * 4 + yy) * 2 + core, tensor)

    up_y, down_y, over_x = at(xl, yp), at(xl, ym), at(xo, y)
    up_z = (dp, lax.rem(z + 1, NZ) * 2 + xh)
    down_z = (dp, lax.rem(z + NZ - 1, NZ) * 2 + xh)
    over_h = (dp, z * 2 + (1 - xh))
    over_c = (p * 2 + (1 - core), tensor)

    half = gw_ref.shape[0]
    cols = gw_ref.shape[1]
    dc = 2 * half
    gate_c, up_c = pl.ds(0, cols), pl.ds(cols, cols)
    n_w = 2 * cols // 256

    barrier = pltpu.get_barrier_semaphore()
    for j in range(1, 8):
        g = lax.rem(p + j, 8)
        pl.semaphore_signal(barrier, inc=1, device_id=(g * 2 + core, tensor), device_id_type=MESH)
    for other in (up_z, down_z, over_h, over_c):
        pl.semaphore_signal(barrier, inc=1, device_id=other, device_id_type=MESH)
    for g in range(8):
        ts[g] = tok_ref[:, g * dc : (g + 1) * dc]
    pl.semaphore_wait(barrier, 11)

    for j in range(1, 8):
        g = lax.rem(p + j, 8)
        send(ts.at[g], ta.at[p], t_send.at[j], t_recv.at[j], (g * 2 + core, tensor))
    mine = pl.ds(pl.multiple_of(core * half, half), half)
    for m, (w_ref, c) in enumerate(((gw_ref, gate_c), (uw_ref, up_c))):
        pltpu.make_async_copy(w_ref, wbuf.at[mine, c], w_local.at[m]).start()
        send(w_ref, wbuf.at[mine, c], w_send.at[m], w_recv.at[m], over_c)
    ta[p] = ts[p]
    for j in range(1, 8):
        take(ta.at[lax.rem(p + 8 - j, 8)], t_recv.at[j])
    send(ta, tb, h_send, h_recv, over_h)
    take(tb, h_recv)
    for g in range(8):
        own, oth = ta[g].astype(F32), tb[g].astype(F32)
        asm[g * 8 : g * 8 + 4] = jnp.where(xh == 0, own, oth)
        asm[g * 8 + 4 : g * 8 + 8] = jnp.where(xh == 0, oth, own)
    xbuf[z] = asm[...].astype(BF16)
    send(xbuf.at[z], xbuf.at[z], az_send.at[0, 0], az_recv.at[0, 0], up_z)
    send(xbuf.at[z], xbuf.at[z], az_send.at[1, 0], az_recv.at[1, 0], down_z)

    theirs = pl.ds(pl.multiple_of((1 - core) * half, half), half)
    for m, c in enumerate((gate_c, up_c)):
        take(wbuf.at[mine, c], w_local.at[m])
        take(wbuf.at[theirs, c], w_recv.at[m])

    def pair_of(s):
        hop = (s + 1) // 2
        sign = 1 - 2 * lax.rem(s + z, 2)
        return lax.rem(z // 2 + sign * hop + NS, NS)

    def gather_z(s):
        lo = lax.rem(z + NZ - 1 - s, NZ)
        hi = lax.rem(z + 1 + s, NZ)
        take(xbuf.at[lo], az_recv.at[0, s])

        @pl.when(s < 7)
        def _():
            send(xbuf.at[lo], xbuf.at[lo], az_send.at[0, s + 1], az_recv.at[0, s + 1], up_z)
            take(xbuf.at[hi], az_recv.at[1, s])

        @pl.when(s < 6)
        def _():
            send(xbuf.at[hi], xbuf.at[hi], az_send.at[1, s + 1], az_recv.at[1, s + 1], down_z)

    def forward(s):
        pair = pair_of(s)
        slot = lax.rem(s, 4)
        x0 = xbuf[2 * pair].astype(F32)
        x1 = xbuf[2 * pair + 1].astype(F32)
        rows = []
        for g in range(8):
            rows += [x0[g * 8 : g * 8 + 8], x1[g * 8 : g * 8 + 8]]
        xf = jnp.concatenate(rows, axis=0)
        xp = xf.astype(BF16)
        for n in range(n_w):
            c = slice(n * 256, (n + 1) * 256)
            part = jnp.dot(xp, wbuf[:, c], preferred_element_type=F32).reshape(2, 4, 16, 256)
            fbuf[slot, :, :, :, c] = part
            sbuf[s, :, :, :, c] = part.astype(BF16)
        send(sbuf.at[s, 0, y2, :, gate_c], gya.at[s, 0], ssem.at[0, s], rsem.at[0, s], up_y)
        send(sbuf.at[s, 1, y2, :, gate_c], gya.at[s, 1], ssem.at[1, s], rsem.at[1, s], down_y)
        send(sbuf.at[s, xo, :, :, up_c], ux.at[s], ssem.at[2, s], rsem.at[2, s], over_x)
        xpt[:, pl.ds(pl.multiple_of(s * 128, 128), 128)] = xf.T.astype(BF16)

    def reduce_b(s):
        slot = lax.rem(s, 4)
        take(gya.at[s, 0], rsem.at[0, s])
        sbuf[s, 0, yp, :, :cols] = (fbuf[slot, 0, yp, :, :cols] + gya[s, 0].astype(F32)).astype(BF16)
        send(sbuf.at[s, :, yp, :, gate_c], gyb.at[s, 0], ssem.at[3, s], rsem.at[3, s], up_y)
        take(gya.at[s, 1], rsem.at[1, s])
        sbuf[s, 1, ym, :, :cols] = (fbuf[slot, 1, ym, :, :cols] + gya[s, 1].astype(F32)).astype(BF16)
        send(sbuf.at[s, :, ym, :, gate_c], gyb.at[s, 1], ssem.at[4, s], rsem.at[4, s], down_y)
        take(ux.at[s], rsem.at[2, s])
        uacc[slot] = fbuf[slot, xl, :, :, cols:] + ux[s].astype(F32)
        us[s, y2] = uacc[slot, y2].astype(BF16)
        send(us.at[s, y2, :, pl.ds(0, CUT)], uya0.at[s], ssem.at[5, s], rsem.at[5, s], up_y)
        send(us.at[s, y2, :, pl.ds(CUT, cols - CUT)], uya1.at[s], ssem.at[6, s], rsem.at[6, s], down_y)

    def reduce_c(s):
        slot = lax.rem(s, 4)
        take(gyb.at[s, 0], rsem.at[3, s])
        take(gyb.at[s, 1], rsem.at[4, s])
        gxs[s] = (
            fbuf[slot, xo, y, :, :cols] + gyb[s, 0, xo].astype(F32) + gyb[s, 1, xo].astype(F32)
        ).astype(BF16)
        send(gxs.at[s], gxr.at[s], ssem.at[7, s], rsem.at[7, s], over_x)
        gown[slot] = fbuf[slot, xl, y, :, :cols] + gyb[s, 0, xl].astype(F32) + gyb[s, 1, xl].astype(F32)
        take(uya0.at[s], rsem.at[5, s])
        us[s, yp, :, :CUT] = (uacc[slot, yp, :, :CUT] + uya0[s].astype(F32)).astype(BF16)
        us[s, yp, :, CUT:] = uacc[slot, yp, :, CUT:].astype(BF16)
        send(us.at[s, yp], uyb.at[s, 0], ssem.at[8, s], rsem.at[8, s], up_y)
        take(uya1.at[s], rsem.at[6, s])
        us[s, ym, :, CUT:] = (uacc[slot, ym, :, CUT:] + uya1[s].astype(F32)).astype(BF16)
        us[s, ym, :, :CUT] = uacc[slot, ym, :, :CUT].astype(BF16)
        send(us.at[s, ym], uyb.at[s, 1], ssem.at[9, s], rsem.at[9, s], down_y)

    def reduce_d(s):
        slot = lax.rem(s, 4)
        rows = pl.ds(pl.multiple_of(pair_of(s) * 16, 16), 16)
        take(gxr.at[s], rsem.at[7, s])
        take(uyb.at[s, 0], rsem.at[8, s])
        take(uyb.at[s, 1], rsem.at[9, s])
        gate = gown[slot] + gxr[s].astype(F32)
        up = uacc[slot, y] + uyb[s, 0].astype(F32) + uyb[s, 1].astype(F32)
        sig = jax.nn.sigmoid(gate)
        act = gate * sig
        hid_ref[rows, :] = (act * up).astype(BF16)
        cot = hg_ref[rows, :].astype(F32)
        dbuf[s, xl, y, :, :cols] = (cot * up * sig * (1.0 + gate * (1.0 - sig))).astype(BF16)
        dbuf[s, xl, y, :, cols:] = (cot * act).astype(BF16)

    def order(i):
        return jnp.where(i < FIRST, i, NS - 1 + FIRST - i)

    def same(ref, kind, s, device):
        send(ref, ref, ssem.at[kind, s], rsem.at[kind, s], device)

    c_lo, c_hi = pl.ds(cols, CUT), pl.ds(cols + CUT, cols - CUT)

    def spread_a(s):
        same(dbuf.at[s, xl, y, :, up_c], 11, s, up_y)
        same(dbuf.at[s, xl, y, :, up_c], 12, s, down_y)
        same(dbuf.at[s, xl, y, :, gate_c], 10, s, over_x)

    def spread_b(s):
        take(dbuf.at[s, xo, y, :, gate_c], rsem.at[10, s])
        same(dbuf.at[s, :, y, :, gate_c], 13, s, up_y)
        same(dbuf.at[s, :, y, :, gate_c], 14, s, down_y)
        take(dbuf.at[s, xl, ym, :, up_c], rsem.at[11, s])
        same(dbuf.at[s, xl, ym, :, c_lo], 15, s, up_y)
        take(dbuf.at[s, xl, yp, :, up_c], rsem.at[12, s])
        same(dbuf.at[s, xl, yp, :, c_hi], 16, s, down_y)

    def spread_c(s):
        take(dbuf.at[s, xl, y2, :, c_lo], rsem.at[15, s])
        take(dbuf.at[s, xl, y2, :, c_hi], rsem.at[16, s])
        same(dbuf.at[s, xl, :, :, up_c], 19, s, over_x)
        take(dbuf.at[s, :, ym, :, gate_c], rsem.at[13, s])
        same(dbuf.at[s, 0, ym, :, gate_c], 17, s, up_y)
        take(dbuf.at[s, :, yp, :, gate_c], rsem.at[14, s])
        same(dbuf.at[s, 1, yp, :, gate_c], 18, s, down_y)

    def spread_d(s):
        take(dbuf.at[s, 0, y2, :, gate_c], rsem.at[17, s])
        take(dbuf.at[s, 1, y2, :, gate_c], rsem.at[18, s])
        take(dbuf.at[s, xo, :, :, up_c], rsem.at[19, s])
        pair = pair_of(s)
        delta = dbuf[s].reshape(128, 2 * cols)
        for n in range(dc // 256):
            c = slice(n * 256, (n + 1) * 256)
            piece = lax.dot_general(
                delta, wbuf[c, :], (((1,), (1,)), ((), ())), preferred_element_type=F32
            )
            for g in range(8):
                for q in range(2):
                    r = g * 16 + q * 8
                    pbuf[2 * pair + q, g * 8 : g * 8 + 8, c] = piece[r : r + 8]

    def ring(side, r, dest, limit, device):
        zacc[...] = pbuf[dest]

        @pl.when(r > 0)
        def _():
            take(zr.at[side, r - 1], z_recv.at[side, r - 1])
            zacc[...] += zr[side, r - 1].astype(F32)

        @pl.when(r - 1 >= limit)
        def _():
            take(zrl.at[side, r - 1 - limit], zl_recv.at[side, r - 1 - limit])
            zacc[...] += zrl[side, r - 1 - limit].astype(F32)

        total = zacc[...]
        top = total.astype(BF16)
        zs[side, r] = top
        send(zs.at[side, r], zr.at[side, r], z_send.at[side, r], z_recv.at[side, r], device)

        @pl.when(r >= limit)
        def _():
            zsl[side, r - limit] = (total - top.astype(F32)).astype(BF16)
            send(
                zsl.at[side, r - limit], zrl.at[side, r - limit],
                zl_send.at[side, r - limit], zl_recv.at[side, r - limit], device,
            )

    def reduce_z(r):
        ring(0, r, lax.rem(z + NZ - 8 + r, NZ), 8 - LOW, down_z)

        @pl.when(r < 7)
        def _():
            ring(1, r, lax.rem(z + 7 - r, NZ), 7 - LOW, up_z)

    def end_z():
        total = pbuf[z]
        for side, last in ((0, 7), (1, 6)):
            take(zr.at[side, last], z_recv.at[side, last])
            total += zr[side, last].astype(F32)
            if LOW:
                take(zrl.at[side, LOW - 1], zl_recv.at[side, LOW - 1])
                total += zrl[side, LOW - 1].astype(F32)
        for g in range(8):
            a, b = total[g * 8 : g * 8 + 4], total[g * 8 + 4 : g * 8 + 8]
            fown[g * 4 : g * 4 + 4] = jnp.where(xh == 0, a, b)
            fs[g * 4 : g * 4 + 4] = jnp.where(xh == 0, b, a)
        send(fs, fr, f_send, f_recv, over_h)

    def end_h():
        take(fr, f_recv)
        total = fown[...] + fr[...]
        for g in range(8):
            ps[g] = total[g * 4 : g * 4 + 4].astype(BF16)
        for j in range(1, 8):
            g = lax.rem(p + j, 8)
            send(ps.at[g], pr.at[p], p_send.at[j], p_recv.at[j], (g * 2 + core, tensor))
        pr[p] = ps[p]

    def weight_tile(w):
        owner = jnp.where(w < 2, 1 - core, core)
        q = lax.rem(w, 2)
        rows = pl.ds(pl.multiple_of(owner * half + q * 256, 256), 256)
        x = xpt[rows, :]
        for n in range(n_w):
            c = slice(n * 256, (n + 1) * 256)
            part = jnp.dot(x, dbuf[:, :, :, :, c].reshape(NS * 128, 256), preferred_element_type=F32)

            @pl.when(w < 2)
            def _():
                ws[q, :, c] = part.astype(BF16)

            @pl.when(w >= 2)
            def _():
                wown[q, :, c] = part

        @pl.when(w < 2)
        def _():
            send(ws.at[q], wr.at[q], ww_send.at[q], ww_recv.at[q], over_c)

    def when(lo, hi, t, body):
        @pl.when(jnp.logical_and(t >= lo, t < hi))
        def _():
            body(t - lo)

    start2 = 10 - FIRST

    def step(t, carry):
        when(0, 8, t, gather_z)
        when(0, 8, t, forward)
        when(1, 9, t, reduce_b)
        when(2, 10, t, reduce_c)
        when(3, 11, t, reduce_d)
        when(start2, start2 + 8, t, lambda i: spread_a(order(i)))
        when(start2 + 1, start2 + 9, t, lambda i: spread_b(order(i)))
        when(start2 + 2, start2 + 10, t, lambda i: spread_c(order(i)))
        when(start2 + 3, start2 + 11, t, lambda i: spread_d(order(i)))
        when(14, 22, t, reduce_z)
        when(22, 23, t, lambda i: end_z())
        when(23, 24, t, lambda i: end_h())
        when(20, 24, t, weight_tile)
        return carry

    lax.fori_loop(0, 24, step, 0)

    for q in range(2):
        take(wr.at[q], ww_recv.at[q])
        rows = slice(q * 256, (q + 1) * 256)
        gg_ref[rows, :] = (wown[q, :, :cols] + wr[q, :, :cols].astype(F32)).astype(BF16)
        ug_ref[rows, :] = (wown[q, :, cols:] + wr[q, :, cols:].astype(F32)).astype(BF16)
    for j in range(1, 8):
        take(pr.at[lax.rem(p + 8 - j, 8)], p_recv.at[j])
    for g in range(8):
        tg_ref[:, g * dc : (g + 1) * dc] = pr[g]

    for j in range(1, 8):
        take(ts.at[0], t_send.at[j])
        take(ps.at[0], p_send.at[j])
    for m, c in enumerate((gate_c, up_c)):
        take(wbuf.at[mine, c], w_send.at[m])
    take(ta, h_send)
    take(fs, f_send)
    for q in range(2):
        take(ws.at[q], ww_send.at[q])

    def drain(s, carry):
        take(xbuf.at[0], az_send.at[0, s])
        take(zs.at[0, s], z_send.at[0, s])

        @pl.when(s < 7)
        def _():
            take(xbuf.at[0], az_send.at[1, s])
            take(zs.at[1, s], z_send.at[1, s])

        for kind, ref in (
            (0, gya.at[s, 0]), (1, gya.at[s, 0]), (2, ux.at[s]), (3, gyb.at[s, 0]), (4, gyb.at[s, 0]),
            (5, uya0.at[s]), (6, uya1.at[s]), (7, gxs.at[s]), (8, us.at[s, 0]), (9, us.at[s, 0]),
            (10, gxs.at[s]), (11, gxs.at[s]), (12, gxs.at[s]), (13, gyb.at[s, 0]), (14, gyb.at[s, 0]),
            (15, uya0.at[s]), (16, uya1.at[s]), (17, gxs.at[s]), (18, gxs.at[s]), (19, ux.at[s]),
        ):
            take(ref, ssem.at[kind, s])
        return carry

    lax.fori_loop(0, NS, drain, 0)
    for side in range(2):
        for s in range(LOW):
            take(zsl.at[side, s], zl_send.at[side, s])


def per_device(tokens, gate_weight, up_weight, hidden_grad):
    half, cols = gate_weight.shape
    rows = tokens.shape[0]
    dc = 2 * half
    group = hidden_grad.shape[0]
    v = pltpu.VMEM
    dma = pltpu.SemaphoreType.DMA
    scratch = [
        v((dc, 2 * cols), BF16),
        v((8, rows, dc), BF16), v((8, rows, dc), BF16), v((8, rows, dc), BF16),
        v((64, dc), F32),
        v((NZ, 64, dc), BF16),
        v((dc, NS * 128), BF16),
        v((NS, 2, 4, 16, 2 * cols), BF16),
        v((4, 2, 4, 16, 2 * cols), F32),
        v((NS, 2, 16, cols), BF16),
        v((NS, 4, 16, cols), BF16),
        v((NS, 2, 2, 16, cols), BF16),
        v((NS, 16, cols), BF16), v((NS, 16, cols), BF16),
        v((4, 16, cols), F32),
        v((4, 4, 16, cols), F32),
        v((NS, 4, 16, cols), BF16),
        v((NS, 16, CUT), BF16), v((NS, 16, cols - CUT), BF16),
        v((NS, 2, 16, cols), BF16),
        v((NS, 2, 4, 16, 2 * cols), BF16),
        v((NZ, 64, dc), F32),
        v((64, dc), F32),
        v((2, 8, 64, dc), BF16), v((2, 8, 64, dc), BF16),
        v((2, LOW, 64, dc), BF16), v((2, LOW, 64, dc), BF16),
        v((32, dc), F32), v((32, dc), F32), v((32, dc), F32),
        v((8, rows, dc), BF16), v((8, rows, dc), BF16),
        v((2, 256, 2 * cols), BF16), v((2, 256, 2 * cols), BF16),
        v((2, 256, 2 * cols), F32),
        dma((2,)), dma((2,)), dma((2,)),
        dma((8,)), dma((8,)),
        dma, dma,
        dma((2, 8)), dma((2, 8)),
        dma((20, NS)), dma((20, NS)),
        dma((2, 8)), dma((2, 8)),
        dma((2, LOW)), dma((2, LOW)),
        dma, dma,
        dma((8,)), dma((8,)),
        dma((2,)), dma((2,)),
    ]
    vm = pl.BlockSpec(memory_space=pltpu.VMEM)
    hbm = pl.BlockSpec(memory_space=pl.ANY)
    return pl.pallas_call(
        kernel,
        out_shape=(
            jax.ShapeDtypeStruct((group, cols), BF16),
            jax.ShapeDtypeStruct(tokens.shape, BF16),
            jax.ShapeDtypeStruct((half, cols), BF16),
            jax.ShapeDtypeStruct((half, cols), BF16),
        ),
        in_specs=[vm, hbm, hbm, vm],
        out_specs=(vm, vm, vm, vm),
        scratch_shapes=scratch,
        compiler_params=pltpu.CompilerParams(
            collective_id=0, has_side_effects=True, vmem_limit_bytes=60 * 1024 * 1024
        ),
        cost_estimate=pl.CostEstimate(flops=11_300_000_000, bytes_accessed=6_000_000, transcendentals=114_688),
    )(tokens, gate_weight, up_weight, hidden_grad)


def solution(mesh):
    placed = (P(("dp", "tensor"), None), P("dp", "tensor"), P("dp", "tensor"), P("dp", "tensor"))
    return jax.shard_map(
        per_device,
        mesh=mesh,
        in_specs=placed,
        out_specs=(
            P("dp", "tensor"),
            P(("dp", "tensor"), None),
            P("dp", "tensor"),
            P("dp", "tensor"),
        ),
        check_vma=False,
    )
```

time: 836 us -> 152 us (0.18)
  the two profiles are of different devices: /device:TPU:8 before, /device:TPU:2 now
where the time goes in v1:
time: 152 us
  Pallas kernels  145 us (95%)
  local copies, waits for them, and re-layouts  5.49 us (4%)
    pallas_call x1, Pallas kernels, per_device(): pl.pallas_call(kernel, out_shape=(jax.ShapeDtypeStruct((group, cols), BF1...  145 us
    unnamed x8, local copies, waits for them, and re-layouts  5.49 us

profile of v1, /device:TPU:2, one launch (start us, length us, event | category | flops | bytes accessed | tf_op | source)
XLA Modules:
  0.0 151.5 jit_solution(18157699073404903623)
XLA Ops:
  0.6 145.4 %shard_map.75 = (bf16[128,896]{1,0:T(8,128)(2,1)}, bf16[4,8192]{1,0:T(4,128)(2,1)}, bf16[512,896]{1,0:T(8,128)(2,1)}, bf16[512,896]{1,0:T(8,128)(2,1)}) custom-call(bf16[4,8192]{1,0:T(4,128)(2,1)} %tok_ref.1, bf16[512,896]{1,0:T(8,128)(2,1)} %gw_ref.1, bf16[512,896]{1,0:T(8,128)(2,1)} %uw_ref.1, bf16[128,896]{1,0:T(8,128)(2,1)} %hg_ref.1), custom_call_target="tpu_custom_call" | custom-call | flops 11299999744 | bytes 6000000 | tf_op jit(solution)/shard_map/pallas_call | solution.py:429
  146.0 0.0 copy-start.1
  146.0 1.7 %copy.12 = bf16[128,896]{1,0:T(8,128)(2,1)} copy(bf16[128,896]{1,0:T(8,128)(2,1)} %get-tuple-element.8) | data formatting | bytes 458752
  147.7 0.0 copy-done.1
  147.7 0.6 copy.13
  148.3 0.0 copy-start
  148.4 2.3 %copy.14 = bf16[512,896]{1,0:T(8,128)(2,1)} copy(bf16[512,896]{1,0:T(8,128)(2,1)} %get-tuple-element.10) | data formatting | bytes 1835008
  150.6 0.0 copy-done
  150.6 0.9 copy.15
Async XLA Ops:
  146.0 1.7 %copy-start.1 = (bf16[4,8192]{1,0:T(4,128)(2,1)S(1)}, bf16[4,8192]{1,0:T(4,128)(2,1)}, u32[]{:S(2)}) copy-start(bf16[4,8192]{1,0:T(4,128)(2,1)} %get-tuple-element.9) | copy-start | bytes 196612
  148.3 2.3 %copy-start = (bf16[512,896]{1,0:T(8,128)(2,1)S(1)}, bf16[512,896]{1,0:T(8,128)(2,1)}, u32[]{:S(2)}) copy-start(bf16[512,896]{1,0:T(8,128)(2,1)} %get-tuple-element.11) | copy-start | bytes 2752516

commit v2 on v0

v2 whole, which is shorter than its diff:
```python
import functools

import jax
import jax.numpy as jnp
from jax import lax
from jax.experimental import pallas as pl
from jax.experimental.pallas import tpu as pltpu
from jax.sharding import PartitionSpec as P

MESH = pl.DeviceIdType.MESH
F32 = jnp.float32
BF16 = jnp.bfloat16
NZ = 16
NS = 8
CY = 768
FIRST = 2
LOW = 2
NU = 4
SUB = 16


def send(src, dst, send_sem, recv_sem, device):
    pltpu.make_async_remote_copy(
        src_ref=src,
        dst_ref=dst,
        send_sem=send_sem,
        recv_sem=recv_sem,
        device_id=device,
        device_id_type=MESH,
    ).start()


def take(ref, sem):
    pltpu.make_async_copy(ref, ref, sem).wait()


def kernel(
    tok_ref, gw_ref, uw_ref, hg_ref,
    hid_ref, tg_ref, gg_ref, ug_ref,
    wbuf, ts, ta, asm, xbuf, xcur, xpt, hgb, hidb,
    sbuf, fbuf, gyb, gxs, gxr, gown, ux, uacc, us, uyb,
    dbuf, pbuf, zacc, zs, zr, zsl, zrl,
    fs, fr, ws, wr, wown, wout,
    l_sem, w_send, w_recv, t_send, t_recv, az_send, az_recv,
    ssem, rsem, z_send, z_recv, zl_send, zl_recv, f_send, f_recv, ww_send, ww_recv, o_sem,
):
    dp, tensor = lax.axis_index("dp"), lax.axis_index("tensor")
    core = lax.rem(dp, 2)
    p = dp // 2
    y, xl = lax.rem(p, 4), p // 4
    xh, z = lax.rem(tensor, 2), tensor // 2
    xo = 1 - xl

    def row_of(k):
        return lax.rem(y + k, 4)

    def at_y(k):
        return ((xl * 4 + row_of(k)) * 2 + core, tensor)

    over_x = ((xo * 4 + y) * 2 + core, tensor)
    up_z = (dp, lax.rem(z + 1, NZ) * 2 + xh)
    down_z = (dp, lax.rem(z + NZ - 1, NZ) * 2 + xh)
    over_c = (p * 2 + (1 - core), tensor)
    plane = [(j, h) for h in range(2) for j in range(8) if j or h]

    def to_plane(j, h):
        g, hh = lax.rem(p + j, 8), lax.rem(xh + h, 2)
        return g, hh, (g * 2 + core, z * 2 + hh)

    half = gw_ref.shape[0]
    cols = gw_ref.shape[1]
    dc = 2 * half
    wide = 2 * cols
    gate_c, up_c = pl.ds(0, cols), pl.ds(cols, cols)
    y_c, x_c = pl.ds(0, CY), pl.ds(CY, wide - CY)

    barrier = pltpu.get_barrier_semaphore()
    for j, h in plane:
        pl.semaphore_signal(barrier, inc=1, device_id=to_plane(j, h)[2], device_id_type=MESH)
    for other in (up_z, down_z, over_c):
        pl.semaphore_signal(barrier, inc=1, device_id=other, device_id_type=MESH)
    mine = pl.ds(pl.multiple_of(core * half, half), half)
    theirs = pl.ds(pl.multiple_of((1 - core) * half, half), half)
    for m, (w_ref, c) in enumerate(((gw_ref, gate_c), (uw_ref, up_c))):
        pltpu.make_async_copy(w_ref, wbuf.at[mine, c], l_sem.at[m]).start()
    pltpu.make_async_copy(hg_ref, hgb, l_sem.at[2]).start()
    for g in range(8):
        ts[g] = tok_ref[:, g * dc : (g + 1) * dc]
    pl.semaphore_wait(barrier, 18)

    for j, h in plane:
        g, hh, device = to_plane(j, h)
        send(ts.at[g], ta.at[xh, p], t_send.at[h, j], t_recv.at[h, j], device)
    for m, (w_ref, c) in enumerate(((gw_ref, gate_c), (uw_ref, up_c))):
        send(w_ref, wbuf.at[mine, c], w_send.at[m], w_recv.at[m], over_c)
    ta[xh, p] = ts[p]
    for j, h in plane:
        take(ta.at[lax.rem(xh + h, 2), lax.rem(p + 8 - j, 8)], t_recv.at[h, j])
    for g in range(8):
        asm[g * 8 : g * 8 + 4] = ta[0, g].astype(F32)
        asm[g * 8 + 4 : g * 8 + 8] = ta[1, g].astype(F32)
    xbuf[z] = asm[...].astype(BF16)

    def block(b, u):
        return xbuf.at[b, pl.ds(u * SUB, SUB), :]

    def send_block(side, b, u, s):
        device = up_z if side == 0 else down_z
        send(block(b, u), block(b, u), az_send.at[side, s, u], az_recv.at[side, s, u], device)

    for u in range(NU):
        send_block(0, z, u, 0)
        send_block(1, z, u, 0)

    for m, c in enumerate((gate_c, up_c)):
        take(wbuf.at[mine, c], l_sem.at[m])
        take(wbuf.at[theirs, c], w_recv.at[m])
    take(hgb, l_sem.at[2])

    def pair_of(s):
        hop = (s + 1) // 2
        sign = 1 - 2 * lax.rem(s + z, 2)
        return lax.rem(z // 2 + sign * hop + NS, NS)

    def gather_z(s, part):
        lo = lax.rem(z + NZ - 1 - s, NZ)
        hi = lax.rem(z + 1 + s, NZ)
        for u in part:
            take(block(lo, u), az_recv.at[0, s, u])

            @pl.when(s < 7)
            def _():
                send_block(0, lo, u, s + 1)
                take(block(hi, u), az_recv.at[1, s, u])

            @pl.when(s < 6)
            def _():
                send_block(1, hi, u, s + 1)

    def rows_of(s):
        pair = pair_of(s)
        x0 = xbuf[2 * pair].astype(F32)
        x1 = xbuf[2 * pair + 1].astype(F32)
        rows = []
        for g in range(8):
            rows += [x0[g * 8 : g * 8 + 8], x1[g * 8 : g * 8 + 8]]
        return jnp.concatenate(rows, axis=0)

    def forward(s, part):
        slot = lax.rem(s, 4)
        if part == 0:
            xp = rows_of(s).astype(BF16)
            xcur[...] = xp
            blocks = range(CY // 256, wide // 256)
        else:
            xp = xcur[...]
            blocks = range(CY // 256)
        for n in blocks:
            c = slice(n * 256, (n + 1) * 256)
            part_sum = jnp.dot(xp, wbuf[:, c], preferred_element_type=F32).reshape(2, 4, 16, 256)
            fbuf[slot, :, :, :, c] = part_sum
            sbuf[s, :, :, :, c] = part_sum.astype(BF16)
        if part == 0:
            send(sbuf.at[s, xo, :, :, x_c], ux.at[s], ssem.at[3, s], rsem.at[3, s], over_x)
        else:
            for k in (1, 2, 3):
                send(
                    sbuf.at[s, :, row_of(k), :, y_c], gyb.at[s, k - 1],
                    ssem.at[k - 1, s], rsem.at[k - 1, s], at_y(k),
                )

    def reduce_b(s):
        slot = lax.rem(s, 4)
        take(ux.at[s], rsem.at[3, s])
        total = fbuf[slot, xl, :, :, CY:] + ux[s].astype(F32)
        uacc[slot] = total
        us[s] = total.astype(BF16)
        for k in (1, 2, 3):
            send(us.at[s, row_of(k)], uyb.at[s, k - 1], ssem.at[4 + k, s], rsem.at[4 + k, s], at_y(k))
        for k in (1, 2, 3):
            take(gyb.at[s, k - 1], rsem.at[k - 1, s])

        def side(xx):
            total = fbuf[slot, xx, y, :, :CY]
            for k in range(3):
                total += gyb[s, k, xx].astype(F32)
            return total

        gxs[s] = side(xo).astype(BF16)
        send(gxs.at[s], gxr.at[s], ssem.at[4, s], rsem.at[4, s], over_x)
        gown[slot] = side(xl)

    def reduce_c(s):
        slot = lax.rem(s, 4)
        rows = pl.ds(pl.multiple_of(pair_of(s) * 16, 16), 16)
        for k in (1, 2, 3):
            take(uyb.at[s, k - 1], rsem.at[4 + k, s])
        take(gxr.at[s], rsem.at[4, s])
        first = gown[slot] + gxr[s].astype(F32)
        second = uacc[slot, y]
        for k in range(3):
            second += uyb[s, k].astype(F32)
        full = jnp.concatenate([first, second], axis=1)
        gate, up = full[:, :cols], full[:, cols:]
        sig = jax.nn.sigmoid(gate)
        act = gate * sig
        hidb[rows, :] = (act * up).astype(BF16)
        cot = hgb[rows, :].astype(F32)
        dbuf[s, xl, y, :, :cols] = (cot * up * sig * (1.0 + gate * (1.0 - sig))).astype(BF16)
        dbuf[s, xl, y, :, cols:] = (cot * act).astype(BF16)

    def order(i):
        return jnp.where(i < FIRST, i, NS - 1 + FIRST - i)

    def same(ref, kind, s, device):
        send(ref, ref, ssem.at[kind, s], rsem.at[kind, s], device)

    def spread_a(s):
        for k in (1, 2, 3):
            same(dbuf.at[s, xl, y, :, x_c], 8 + k, s, at_y(k))
        same(dbuf.at[s, xl, y, :, y_c], 8, s, over_x)

    def spread_b(s):
        take(dbuf.at[s, xo, y, :, y_c], rsem.at[8, s])
        for k in (1, 2, 3):
            same(dbuf.at[s, :, y, :, y_c], 11 + k, s, at_y(k))
        for k in (1, 2, 3):
            take(dbuf.at[s, xl, row_of(4 - k), :, x_c], rsem.at[8 + k, s])
        same(dbuf.at[s, xl, :, :, x_c], 15, s, over_x)

    def spread_c(s, part):
        if part == 0:
            for k in (1, 2, 3):
                take(dbuf.at[s, :, row_of(4 - k), :, y_c], rsem.at[11 + k, s])
            take(dbuf.at[s, xo, :, :, x_c], rsem.at[15, s])
        pair = pair_of(s)
        delta = dbuf[s].reshape(128, wide)
        width = dc // 2
        for n in range(part * width // 256, (part + 1) * width // 256):
            c = slice(n * 256, (n + 1) * 256)
            piece = lax.dot_general(
                delta, wbuf[c, :], (((1,), (1,)), ((), ())), preferred_element_type=F32
            )
            for g in range(8):
                for q in range(2):
                    r = g * 16 + q * 8
                    pbuf[2 * pair + q, g * 8 : g * 8 + 8, c] = piece[r : r + 8]

    def ring(side, r, u):
        dest = lax.rem(z + NZ - 8 + r, NZ) if side == 0 else lax.rem(z + 7 - r, NZ)
        limit = (8 if side == 0 else 7) - LOW
        device = down_z if side == 0 else up_z
        rows = pl.ds(u * SUB, SUB)
        zacc[...] = pbuf[dest, rows, :]

        @pl.when(r > 0)
        def _():
            take(zr.at[side, r - 1, rows], z_recv.at[side, r - 1, u])
            zacc[...] += zr[side, r - 1, rows].astype(F32)

        @pl.when(r - 1 >= limit)
        def _():
            take(zrl.at[side, r - 1 - limit, rows], zl_recv.at[side, r - 1 - limit, u])
            zacc[...] += zrl[side, r - 1 - limit, rows].astype(F32)

        total = zacc[...]
        top = total.astype(BF16)
        zs[side, r, rows] = top
        send(zs.at[side, r, rows], zr.at[side, r, rows], z_send.at[side, r, u], z_recv.at[side, r, u], device)

        @pl.when(r >= limit)
        def _():
            zsl[side, r - limit, rows] = (total - top.astype(F32)).astype(BF16)
            send(
                zsl.at[side, r - limit, rows], zrl.at[side, r - limit, rows],
                zl_send.at[side, r - limit, u], zl_recv.at[side, r - limit, u], device,
            )

    def reduce_z(r, part):
        for u in part:
            ring(0, r, u)

            @pl.when(r > 0)
            def _():
                ring(1, r - 1, u)

    def end_z():
        for u in range(NU):
            rows = pl.ds(u * SUB, SUB)
            total = pbuf[z, rows, :]
            for side, last in ((0, 7), (1, 6)):
                take(zr.at[side, last, rows], z_recv.at[side, last, u])
                total += zr[side, last, rows].astype(F32)
                take(zrl.at[side, LOW - 1, rows], zl_recv.at[side, LOW - 1, u])
                total += zrl[side, LOW - 1, rows].astype(F32)
            for i in range(SUB // 8):
                g = u * (SUB // 8) + i
                fs[0, g] = total[i * 8 : i * 8 + 4]
                fs[1, g] = total[i * 8 + 4 : i * 8 + 8]
        for j, h in plane:
            g, hh, device = to_plane(j, h)
            send(fs.at[hh, g], fr.at[xh, p], f_send.at[h, j], f_recv.at[h, j], device)
        fr[xh, p] = fs[xh, p]

    def turn(s):
        xpt[:, pl.ds(pl.multiple_of(s * 128, 128), 128)] = rows_of(s).T.astype(BF16)

    def weight_tile(w, part):
        owner = jnp.where(w < 2, 1 - core, core)
        q = lax.rem(w, 2)
        rows = pl.ds(pl.multiple_of(owner * half + q * 256, 256), 256)
        x = xpt[rows, :]
        for n in range(4) if part == 0 else range(4, wide // 256):
            c = slice(n * 256, (n + 1) * 256)
            total = jnp.dot(x, dbuf[:, :, :, :, c].reshape(NS * 128, 256), preferred_element_type=F32)

            @pl.when(w < 2)
            def _():
                ws[q, :, c] = total.astype(BF16)

            @pl.when(w >= 2)
            def _():
                wown[q, :, c] = total

        if part == 1:

            @pl.when(w < 2)
            def _():
                send(ws.at[q], wr.at[q], ww_send.at[q], ww_recv.at[q], over_c)

    def when(lo, hi, t, body):
        @pl.when(jnp.logical_and(t >= lo, t < hi))
        def _():
            body(t - lo)

    start2 = 12 - FIRST

    def gather_at(t, u):
        when(0, 8, t, lambda s: gather_z(s, range(u, u + 1)))

    def ring_at(t, u):
        when(15, 23, t, lambda r: reduce_z(r, range(u, u + 1)))

    def step(t, carry):
        ring_at(t, 0)
        gather_at(t, 0)
        when(5, 13, t, reduce_c)
        when(start2, start2 + 8, t, lambda i: spread_a(order(i)))
        gather_at(t, 1)
        when(3, 11, t, reduce_b)
        when(start2 + 1, start2 + 9, t, lambda i: spread_b(order(i)))
        ring_at(t, 1)
        gather_at(t, 2)
        when(1, 9, t, lambda s: forward(s, 0))
        when(start2 + 2, start2 + 10, t, lambda i: spread_c(order(i), 0))
        when(20, 24, t, lambda w: weight_tile(w, 0))
        ring_at(t, 2)
        gather_at(t, 3)
        when(1, 9, t, lambda s: forward(s, 1))
        when(start2 + 2, start2 + 10, t, lambda i: spread_c(order(i), 1))
        ring_at(t, 3)
        when(23, 24, t, lambda i: end_z())
        when(20, 24, t, lambda w: weight_tile(w, 1))
        when(8, 16, t, turn)
        return carry

    lax.fori_loop(0, 24, step, 0)

    pltpu.make_async_copy(hidb, hid_ref, o_sem.at[0]).start()
    for q in range(2):
        take(wr.at[q], ww_recv.at[q])
        wout[q] = (wown[q] + wr[q].astype(F32)).astype(BF16)
        rows = pl.ds(q * 256, 256)
        pltpu.make_async_copy(wout.at[q, :, gate_c], gg_ref.at[rows, :], o_sem.at[1 + q]).start()
        pltpu.make_async_copy(wout.at[q, :, up_c], ug_ref.at[rows, :], o_sem.at[3 + q]).start()
    for j, h in plane:
        take(fr.at[lax.rem(xh + h, 2), lax.rem(p + 8 - j, 8)], f_recv.at[h, j])
    for g in range(8):
        tg_ref[:, g * dc : (g + 1) * dc] = (fr[0, g] + fr[1, g]).astype(BF16)

    for j, h in plane:
        take(ts.at[0], t_send.at[h, j])
        take(fs.at[0, 0], f_send.at[h, j])
    for m, c in enumerate((gate_c, up_c)):
        take(wbuf.at[mine, c], w_send.at[m])
    for q in range(2):
        take(ws.at[q], ww_send.at[q])

    def drain(s, carry):
        for u in range(NU):
            take(block(0, u), az_send.at[0, s, u])
            take(zs.at[0, s, pl.ds(u * SUB, SUB)], z_send.at[0, s, u])

            @pl.when(s < 7)
            def _():
                take(block(0, u), az_send.at[1, s, u])
                take(zs.at[1, s, pl.ds(u * SUB, SUB)], z_send.at[1, s, u])

            @pl.when(s < LOW)
            def _():
                for side in range(2):
                    take(zsl.at[side, s, pl.ds(u * SUB, SUB)], zl_send.at[side, s, u])

        for k in range(3):
            take(gyb.at[s, k], ssem.at[k, s])
            take(uyb.at[s, k], ssem.at[5 + k, s])
            take(uyb.at[s, k], ssem.at[9 + k, s])
            take(gyb.at[s, k], ssem.at[12 + k, s])
        take(ux.at[s], ssem.at[3, s])
        take(gxs.at[s], ssem.at[4, s])
        take(gxs.at[s], ssem.at[8, s])
        take(ux.at[s], ssem.at[15, s])
        return carry

    lax.fori_loop(0, NS, drain, 0)
    take(hidb, o_sem.at[0])
    for q in range(2):
        take(wout.at[q, :, gate_c], o_sem.at[1 + q])
        take(wout.at[q, :, up_c], o_sem.at[3 + q])


def per_device(tokens, gate_weight, up_weight, hidden_grad):
    half, cols = gate_weight.shape
    rows = tokens.shape[0]
    dc = 2 * half
    wide = 2 * cols
    cx = wide - CY
    group = hidden_grad.shape[0]
    v = pltpu.VMEM
    dma = pltpu.SemaphoreType.DMA
    scratch = [
        v((dc, wide), BF16),
        v((8, rows, dc), BF16), v((2, 8, rows, dc), BF16),
        v((64, dc), F32),
        v((NZ, 64, dc), BF16),
        v((128, dc), BF16),
        v((dc, NS * 128), BF16),
        v((group, cols), BF16), v((group, cols), BF16),
        v((NS, 2, 4, 16, wide), BF16),
        v((4, 2, 4, 16, wide), F32),
        v((NS, 3, 2, 16, CY), BF16),
        v((NS, 16, CY), BF16), v((NS, 16, CY), BF16),
        v((4, 16, CY), F32),
        v((NS, 4, 16, cx), BF16),
        v((4, 4, 16, cx), F32),
        v((NS, 4, 16, cx), BF16),
        v((NS, 3, 16, cx), BF16),
        v((NS, 2, 4, 16, wide), BF16),
        v((NZ, 64, dc), F32),
        v((SUB, dc), F32),
        v((2, 8, 64, dc), BF16), v((2, 8, 64, dc), BF16),
        v((2, LOW, 64, dc), BF16), v((2, LOW, 64, dc), BF16),
        v((2, 8, rows, dc), F32), v((2, 8, rows, dc), F32),
        v((2, 256, wide), BF16), v((2, 256, wide), BF16),
        v((2, 256, wide), F32),
        v((2, 256, wide), BF16),
        dma((3,)), dma((2,)), dma((2,)),
        dma((2, 8)), dma((2, 8)),
        dma((2, 8, NU)), dma((2, 8, NU)),
        dma((16, NS)), dma((16, NS)),
        dma((2, 8, NU)), dma((2, 8, NU)),
        dma((2, LOW, NU)), dma((2, LOW, NU)),
        dma((2, 8)), dma((2, 8)),
        dma((2,)), dma((2,)),
        dma((5,)),
    ]
    vm = pl.BlockSpec(memory_space=pltpu.VMEM)
    hbm = pl.BlockSpec(memory_space=pl.ANY)
    return pl.pallas_call(
        kernel,
        out_shape=(
            jax.ShapeDtypeStruct((group, cols), BF16),
            jax.ShapeDtypeStruct(tokens.shape, BF16),
            jax.ShapeDtypeStruct((half, cols), BF16),
            jax.ShapeDtypeStruct((half, cols), BF16),
        ),
        in_specs=[vm, hbm, hbm, hbm],
        out_specs=(hbm, vm, hbm, hbm),
        scratch_shapes=scratch,
        compiler_params=pltpu.CompilerParams(
            collective_id=0, has_side_effects=True, vmem_limit_bytes=60 * 1024 * 1024
        ),
        cost_estimate=pl.CostEstimate(flops=11_300_000_000, bytes_accessed=6_000_000, transcendentals=114_688),
    )(tokens, gate_weight, up_weight, hidden_grad)


def solution(mesh):
    placed = (P(("dp", "tensor"), None), P("dp", "tensor"), P("dp", "tensor"), P("dp", "tensor"))
    return jax.shard_map(
        per_device,
        mesh=mesh,
        in_specs=placed,
        out_specs=(
            P("dp", "tensor"),
            P(("dp", "tensor"), None),
            P("dp", "tensor"),
            P("dp", "tensor"),
        ),
        check_vma=False,
    )
```

time: 836 us -> 132 us (0.16)
  waiting for transfers between devices: 492 us -> 0 us
  blocking collectives: 248 us -> 0 us
  Pallas kernels: 0 us -> 126 us
  matrix products: 35.1 us -> 0 us
  starting transfers between devices: 20.5 us -> 0 us
  between operations: 14.4 us -> 0.65 us
  local copies, waits for them, and re-layouts: 15.6 us -> 5.49 us
  other arithmetic: 9.89 us -> 0 us
    all_to_all x3 -> x0, waiting for transfers between devices: 253 us -> none  [the longest x1 106 us: per_device(): lax.all_to_all(part_gate, 'dp', split_axis=0, concat_axis=1, tiled=True)]
    all_gather x3 -> x0, waiting for transfers between devices: 238 us -> none  [the longest x1 158 us: per_device(): rows = lax.all_gather(tokens, 'tensor', axis=0, tiled=True)]
    unnamed x1 -> x0, blocking collectives: 219 us -> none
    pallas_call x0 -> x1, Pallas kernels: none -> 126 us  [per_device(): pl.pallas_call(kernel, out_shape=(jax.ShapeDtypeStruct((group, cols), BF1...]
    dot_general x6 -> x0, matrix products: 35.1 us -> none  [the longest x1 7.95 us: per_device(): lax.dot_general(all_up, up_weight, contract_cols, preferred_element_type=...]
    all_to_all x1 -> x0, blocking collectives: 28.9 us -> none  [per_device(): slices = lax.all_to_all(rows, 'dp', split_axis=1, concat_axis=0, tiled=True)]
    all_to_all x3 -> x0, starting transfers between devices: 20.3 us -> none  [the longest x1 7.95 us: per_device(): lax.all_to_all(part_up, 'dp', split_axis=0, concat_axis=1, tiled=True)]
    all_to_all x3 -> x0, local copies, waits for them, and re-layouts: 9.23 us -> none  [the longest x1 4.8 us: per_device(): lax.all_to_all(pieces, 'dp', split_axis=0, concat_axis=1, tiled=True)]
  transfers between devices with their start and end apart: 6 -> 0, of which waited for: 6 -> 0; matrix products, arithmetic and copies ran while one was open for 4% -> 0% of each run, Pallas kernels for 0% -> 0%
where the time goes in v2:
time: 132 us
  Pallas kernels  126 us (95%)
  local copies, waits for them, and re-layouts  5.49 us (4%)
    pallas_call x1, Pallas kernels, per_device(): pl.pallas_call(kernel, out_shape=(jax.ShapeDtypeStruct((group, cols), BF1...  126 us
    unnamed x8, local copies, waits for them, and re-layouts  5.49 us

profile of v2, /device:TPU:8, one launch (start us, length us, event | category | flops | bytes accessed | tf_op | source)
XLA Modules:
  0.0 131.7 jit_solution(218546923553906383)
XLA Ops:
  0.6 125.6 %shard_map.75 = (bf16[128,896]{1,0:T(8,128)(2,1)}, bf16[4,8192]{1,0:T(4,128)(2,1)}, bf16[512,896]{1,0:T(8,128)(2,1)}, bf16[512,896]{1,0:T(8,128)(2,1)}) custom-call(bf16[4,8192]{1,0:T(4,128)(2,1)} %tok_ref.1, bf16[512,896]{1,0:T(8,128)(2,1)} %gw_ref.1, bf16[512,896]{1,0:T(8,128)(2,1)} %uw_ref.1, bf16[128,896]{1,0:T(8,128)(2,1)} %hg_ref.1), custom_call_target="tpu_custom_call" | custom-call | flops 11299999744 | bytes 6000000 | tf_op jit(solution)/shard_map/pallas_call | solution.py:469
  126.2 0.0 copy-start.1
  126.2 1.7 %copy.12 = bf16[128,896]{1,0:T(8,128)(2,1)} copy(bf16[128,896]{1,0:T(8,128)(2,1)} %get-tuple-element.8) | data formatting | bytes 458752
  127.9 0.0 copy-done.1
  127.9 0.6 copy.13
  128.5 0.0 copy-start
  128.5 2.3 %copy.14 = bf16[512,896]{1,0:T(8,128)(2,1)} copy(bf16[512,896]{1,0:T(8,128)(2,1)} %get-tuple-element.10) | data formatting | bytes 1835008
  130.8 0.0 copy-done
  130.8 0.9 copy.15
Async XLA Ops:
  126.2 1.7 %copy-start.1 = (bf16[4,8192]{1,0:T(4,128)(2,1)S(1)}, bf16[4,8192]{1,0:T(4,128)(2,1)}, u32[]{:S(2)}) copy-start(bf16[4,8192]{1,0:T(4,128)(2,1)} %get-tuple-element.9) | copy-start | bytes 196612
  128.5 2.3 %copy-start = (bf16[512,896]{1,0:T(8,128)(2,1)S(1)}, bf16[512,896]{1,0:T(8,128)(2,1)}, u32[]{:S(2)}) copy-start(bf16[512,896]{1,0:T(8,128)(2,1)} %get-tuple-element.11) | copy-start | bytes 2752516

commit v3 on v2

--- a/solution.py
+++ b/solution.py
@@ -13,7 +13,7 @@
 NZ = 16
 NS = 8
 CY = 768
-FIRST = 2
+FIRST = 0
 LOW = 2
 NU = 4
 SUB = 16
@@ -91,9 +91,10 @@
     for j, h in plane:
         g, hh, device = to_plane(j, h)
         send(ts.at[g], ta.at[xh, p], t_send.at[h, j], t_recv.at[h, j], device)
-    for m, (w_ref, c) in enumerate(((gw_ref, gate_c), (uw_ref, up_c))):
-        send(w_ref, wbuf.at[mine, c], w_send.at[m], w_recv.at[m], over_c)
     ta[xh, p] = ts[p]
+    for m, c in enumerate((gate_c, up_c)):
+        take(wbuf.at[mine, c], l_sem.at[m])
+        send(wbuf.at[mine, c], wbuf.at[mine, c], w_send.at[m], w_recv.at[m], over_c)
     for j, h in plane:
         take(ta.at[lax.rem(xh + h, 2), lax.rem(p + 8 - j, 8)], t_recv.at[h, j])
     for g in range(8):
@@ -112,10 +113,6 @@
         send_block(0, z, u, 0)
         send_block(1, z, u, 0)
 
-    for m, c in enumerate((gate_c, up_c)):
-        take(wbuf.at[mine, c], l_sem.at[m])
-        take(wbuf.at[theirs, c], w_recv.at[m])
-    take(hgb, l_sem.at[2])
 
     def pair_of(s):
         hop = (s + 1) // 2
@@ -149,11 +146,18 @@
     def forward(s, part):
         slot = lax.rem(s, 4)
         if part == 0:
+
+            @pl.when(s == 0)
+            def _():
+                for m, c in enumerate((gate_c, up_c)):
+                    take(wbuf.at[theirs, c], w_recv.at[m])
+                take(hgb, l_sem.at[2])
+
             xp = rows_of(s).astype(BF16)
-            xcur[...] = xp
+            xcur[s] = xp
             blocks = range(CY // 256, wide // 256)
         else:
-            xp = xcur[...]
+            xp = xcur[s]
             blocks = range(CY // 256)
         for n in blocks:
             c = slice(n * 256, (n + 1) * 256)
@@ -216,9 +220,9 @@
         send(ref, ref, ssem.at[kind, s], rsem.at[kind, s], device)
 
     def spread_a(s):
+        same(dbuf.at[s, xl, y, :, y_c], 8, s, over_x)
         for k in (1, 2, 3):
             same(dbuf.at[s, xl, y, :, x_c], 8 + k, s, at_y(k))
-        same(dbuf.at[s, xl, y, :, y_c], 8, s, over_x)
 
     def spread_b(s):
         take(dbuf.at[s, xo, y, :, y_c], rsem.at[8, s])
@@ -303,7 +307,7 @@
         fr[xh, p] = fs[xh, p]
 
     def turn(s):
-        xpt[:, pl.ds(pl.multiple_of(s * 128, 128), 128)] = rows_of(s).T.astype(BF16)
+        xpt[:, pl.ds(pl.multiple_of(s * 128, 128), 128)] = xcur[s].T
 
     def weight_tile(w, part):
         owner = jnp.where(w < 2, 1 - core, core)
@@ -353,18 +357,18 @@
         gather_at(t, 2)
         when(1, 9, t, lambda s: forward(s, 0))
         when(start2 + 2, start2 + 10, t, lambda i: spread_c(order(i), 0))
-        when(20, 24, t, lambda w: weight_tile(w, 0))
+        when(22 - FIRST, 26 - FIRST, t, lambda w: weight_tile(w, 0))
         ring_at(t, 2)
         gather_at(t, 3)
         when(1, 9, t, lambda s: forward(s, 1))
         when(start2 + 2, start2 + 10, t, lambda i: spread_c(order(i), 1))
         ring_at(t, 3)
         when(23, 24, t, lambda i: end_z())
-        when(20, 24, t, lambda w: weight_tile(w, 1))
+        when(22 - FIRST, 26 - FIRST, t, lambda w: weight_tile(w, 1))
         when(8, 16, t, turn)
         return carry
 
-    lax.fori_loop(0, 24, step, 0)
+    lax.fori_loop(0, max(24, 26 - FIRST), step, 0)
 
     pltpu.make_async_copy(hidb, hid_ref, o_sem.at[0]).start()
     for q in range(2):
@@ -417,6 +421,11 @@
     for q in range(2):
         take(wout.at[q, :, gate_c], o_sem.at[1 + q])
         take(wout.at[q, :, up_c], o_sem.at[3 + q])
+
+
+def finish(*refs):
+    for src, dst in zip(refs[:4], refs[4:]):
+        dst[...] = src[...]
 
 
 def per_device(tokens, gate_weight, up_weight, hidden_grad):
@@ -433,7 +442,7 @@
         v((8, rows, dc), BF16), v((2, 8, rows, dc), BF16),
         v((64, dc), F32),
         v((NZ, 64, dc), BF16),
-        v((128, dc), BF16),
+        v((NS, 128, dc), BF16),
         v((dc, NS * 128), BF16),
         v((group, cols), BF16), v((group, cols), BF16),
         v((NS, 2, 4, 16, wide), BF16),
@@ -466,14 +475,15 @@
     ]
     vm = pl.BlockSpec(memory_space=pltpu.VMEM)
     hbm = pl.BlockSpec(memory_space=pl.ANY)
-    return pl.pallas_call(
+    shapes = (
+        jax.ShapeDtypeStruct((group, cols), BF16),
+        jax.ShapeDtypeStruct(tokens.shape, BF16),
+        jax.ShapeDtypeStruct((half, cols), BF16),
+        jax.ShapeDtypeStruct((half, cols), BF16),
+    )
+    results = pl.pallas_call(
         kernel,
-        out_shape=(
-            jax.ShapeDtypeStruct((group, cols), BF16),
-            jax.ShapeDtypeStruct(tokens.shape, BF16),
-            jax.ShapeDtypeStruct((half, cols), BF16),
-            jax.ShapeDtypeStruct((half, cols), BF16),
-        ),
+        out_shape=shapes,
         in_specs=[vm, hbm, hbm, hbm],
         out_specs=(hbm, vm, hbm, hbm),
         scratch_shapes=scratch,
@@ -482,6 +492,12 @@
         ),
         cost_estimate=pl.CostEstimate(flops=11_300_000_000, bytes_accessed=6_000_000, transcendentals=114_688),
     )(tokens, gate_weight, up_weight, hidden_grad)
+    return pl.pallas_call(
+        finish,
+        out_shape=shapes,
+        in_specs=[vm] * 4,
+        out_specs=(vm,) * 4,
+    )(*results)
 
 
 def solution(mesh):

time: 132 us -> 125 us (0.947)
  the two profiles are of different devices: /device:TPU:8 before, /device:TPU:2 now
where the time goes in v3:
time: 125 us
  Pallas kernels  125 us (100%)
    pallas_call x1, Pallas kernels, per_device(): pl.pallas_call(kernel, out_shape=shapes, in_specs=[vm, hbm, hbm, hbm], ou...  122 us
    pallas_call x1, Pallas kernels, per_device(): pl.pallas_call(finish, out_shape=shapes, in_specs=[vm] * 4, out_specs=(vm...  3 us

profile of v3, /device:TPU:2, one launch (start us, length us, event | category | flops | bytes accessed | tf_op | source)
XLA Modules:
  0.0 125.3 jit_solution(12394983500358874757)
XLA Ops:
  0.6 121.6 %shard_map.75 = (bf16[128,896]{1,0:T(8,128)(2,1)}, bf16[4,8192]{1,0:T(4,128)(2,1)}, bf16[512,896]{1,0:T(8,128)(2,1)}, bf16[512,896]{1,0:T(8,128)(2,1)}) custom-call(bf16[4,8192]{1,0:T(4,128)(2,1)} %tok_ref.1, bf16[512,896]{1,0:T(8,128)(2,1)} %gw_ref.1, bf16[512,896]{1,0:T(8,128)(2,1)} %uw_ref.1, bf16[128,896]{1,0:T(8,128)(2,1)} %hg_ref.1), custom_call_target="tpu_custom_call" | custom-call | flops 11299999744 | bytes 6000000 | tf_op jit(solution)/shard_map/pallas_call | solution.py:484
  122.3 3.0 %shard_map.76 = (bf16[128,896]{1,0:T(8,128)(2,1)}, bf16[4,8192]{1,0:T(4,128)(2,1)}, bf16[512,896]{1,0:T(8,128)(2,1)}, bf16[512,896]{1,0:T(8,128)(2,1)}) custom-call(bf16[128,896]{1,0:T(8,128)(2,1)} %get-tuple-element.8.refs_0_, bf16[4,8192]{1,0:T(4,128)(2,1)} %get-tuple-element.9.refs_1_, bf16[512,896]{1,0:T(8,128)(2,1)} %get-tuple-element.10.refs_2_, ...), custom_call_target="tpu_custom_call" | custom-call | tf_op jit(solution)/shard_map/pallas_call | solution.py:495

commit v4 on v3

--- a/solution.py
+++ b/solution.py
@@ -15,6 +15,7 @@
 CY = 768
 FIRST = 0
 LOW = 2
+TURNS = 3
 NU = 4
 SUB = 16
 
@@ -37,7 +38,7 @@
 def kernel(
     tok_ref, gw_ref, uw_ref, hg_ref,
     hid_ref, tg_ref, gg_ref, ug_ref,
-    wbuf, ts, ta, asm, xbuf, xcur, xpt, hgb, hidb,
+    wbuf, wt, ts, ta, asm, xbuf, xcur, xpt, hgb, hidb,
     sbuf, fbuf, gyb, gxs, gxr, gown, ux, uacc, us, uyb,
     dbuf, pbuf, zacc, zs, zr, zsl, zrl,
     fs, fr, ws, wr, wown, wout,
@@ -243,7 +244,7 @@
         for n in range(part * width // 256, (part + 1) * width // 256):
             c = slice(n * 256, (n + 1) * 256)
             piece = lax.dot_general(
-                delta, wbuf[c, :], (((1,), (1,)), ((), ())), preferred_element_type=F32
+                delta, wt[:, c], (((1,), (0,)), ((), ())), preferred_element_type=F32
             )
             for g in range(8):
                 for q in range(2):
@@ -309,28 +310,38 @@
     def turn(s):
         xpt[:, pl.ds(pl.multiple_of(s * 128, 128), 128)] = xcur[s].T
 
-    def weight_tile(w, part):
-        owner = jnp.where(w < 2, 1 - core, core)
-        q = lax.rem(w, 2)
-        rows = pl.ds(pl.multiple_of(owner * half + q * 256, 256), 256)
-        x = xpt[rows, :]
-        for n in range(4) if part == 0 else range(4, wide // 256):
+    w_part = (pl.ds(0, 1024), pl.ds(1024, wide - 1024))
+
+    def weight_half(w):
+        owner = jnp.where(w == 0, 1 - core, core)
+        x = xpt[pl.ds(pl.multiple_of(owner * half, half), half), :]
+        for n in range(wide // 256):
             c = slice(n * 256, (n + 1) * 256)
             total = jnp.dot(x, dbuf[:, :, :, :, c].reshape(NS * 128, 256), preferred_element_type=F32)
 
-            @pl.when(w < 2)
-            def _():
-                ws[q, :, c] = total.astype(BF16)
-
-            @pl.when(w >= 2)
-            def _():
-                wown[q, :, c] = total
-
-        if part == 1:
-
-            @pl.when(w < 2)
-            def _():
-                send(ws.at[q], wr.at[q], ww_send.at[q], ww_recv.at[q], over_c)
+            @pl.when(w == 0)
+            def _():
+                ws[:, c] = total.astype(BF16)
+
+            @pl.when(w == 1)
+            def _():
+                wown[:, c] = total
+
+            if n in (3, wide // 256 - 1):
+                q = 0 if n == 3 else 1
+
+                @pl.when(w == 0)
+                def _():
+                    send(ws.at[:, w_part[q]], wr.at[:, w_part[q]], ww_send.at[q], ww_recv.at[q], over_c)
+
+    def turn_weights(i):
+        for k in range(TURNS):
+            n = i * TURNS + k
+
+            @pl.when(n < wide // 128)
+            def _():
+                c = pl.ds(pl.multiple_of(n * 128, 128), 128)
+                wt[c, :] = wbuf[:, c].T
 
     def when(lo, hi, t, body):
         @pl.when(jnp.logical_and(t >= lo, t < hi))
@@ -357,26 +368,26 @@
         gather_at(t, 2)
         when(1, 9, t, lambda s: forward(s, 0))
         when(start2 + 2, start2 + 10, t, lambda i: spread_c(order(i), 0))
-        when(22 - FIRST, 26 - FIRST, t, lambda w: weight_tile(w, 0))
         ring_at(t, 2)
         gather_at(t, 3)
         when(1, 9, t, lambda s: forward(s, 1))
         when(start2 + 2, start2 + 10, t, lambda i: spread_c(order(i), 1))
         ring_at(t, 3)
         when(23, 24, t, lambda i: end_z())
-        when(22 - FIRST, 26 - FIRST, t, lambda w: weight_tile(w, 1))
+        when(22, 24, t, weight_half)
         when(8, 16, t, turn)
+        when(9, 14, t, turn_weights)
         return carry
 
-    lax.fori_loop(0, max(24, 26 - FIRST), step, 0)
+    lax.fori_loop(0, 24, step, 0)
 
     pltpu.make_async_copy(hidb, hid_ref, o_sem.at[0]).start()
     for q in range(2):
-        take(wr.at[q], ww_recv.at[q])
-        wout[q] = (wown[q] + wr[q].astype(F32)).astype(BF16)
-        rows = pl.ds(q * 256, 256)
-        pltpu.make_async_copy(wout.at[q, :, gate_c], gg_ref.at[rows, :], o_sem.at[1 + q]).start()
-        pltpu.make_async_copy(wout.at[q, :, up_c], ug_ref.at[rows, :], o_sem.at[3 + q]).start()
+        take(wr.at[:, w_part[q]], ww_recv.at[q])
+        wout[:, w_part[q]] = (wown[:, w_part[q]] + wr[:, w_part[q]].astype(F32)).astype(BF16)
+        if q == 0:
+            pltpu.make_async_copy(wout.at[:, gate_c], gg_ref, o_sem.at[1]).start()
+    pltpu.make_async_copy(wout.at[:, up_c], ug_ref, o_sem.at[2]).start()
     for j, h in plane:
         take(fr.at[lax.rem(xh + h, 2), lax.rem(p + 8 - j, 8)], f_recv.at[h, j])
     for g in range(8):
@@ -388,7 +399,7 @@
     for m, c in enumerate((gate_c, up_c)):
         take(wbuf.at[mine, c], w_send.at[m])
     for q in range(2):
-        take(ws.at[q], ww_send.at[q])
+        take(ws.at[:, w_part[q]], ww_send.at[q])
 
     def drain(s, carry):
         for u in range(NU):
@@ -418,9 +429,8 @@
 
     lax.fori_loop(0, NS, drain, 0)
     take(hidb, o_sem.at[0])
-    for q in range(2):
-        take(wout.at[q, :, gate_c], o_sem.at[1 + q])
-        take(wout.at[q, :, up_c], o_sem.at[3 + q])
+    take(wout.at[:, gate_c], o_sem.at[1])
+    take(wout.at[:, up_c], o_sem.at[2])
 
 
 def finish(*refs):
@@ -439,6 +449,7 @@
     dma = pltpu.SemaphoreType.DMA
     scratch = [
         v((dc, wide), BF16),
+        v((wide, dc), BF16),
         v((8, rows, dc), BF16), v((2, 8, rows, dc), BF16),
         v((64, dc), F32),
         v((NZ, 64, dc), BF16),
@@ -460,9 +471,9 @@
         v((2, 8, 64, dc), BF16), v((2, 8, 64, dc), BF16),
         v((2, LOW, 64, dc), BF16), v((2, LOW, 64, dc), BF16),
         v((2, 8, rows, dc), F32), v((2, 8, rows, dc), F32),
-        v((2, 256, wide), BF16), v((2, 256, wide), BF16),
-        v((2, 256, wide), F32),
-        v((2, 256, wide), BF16),
+        v((half, wide), BF16), v((half, wide), BF16),
+        v((half, wide), F32),
+        v((half, wide), BF16),
         dma((3,)), dma((2,)), dma((2,)),
         dma((2, 8)), dma((2, 8)),
         dma((2, 8, NU)), dma((2, 8, NU)),
@@ -471,7 +482,7 @@
         dma((2, LOW, NU)), dma((2, LOW, NU)),
         dma((2, 8)), dma((2, 8)),
         dma((2,)), dma((2,)),
-        dma((5,)),
+        dma((3,)),
     ]
     vm = pl.BlockSpec(memory_space=pltpu.VMEM)
     hbm = pl.BlockSpec(memory_space=pl.ANY)

time: 125 us -> 123 us (0.984)
  the two profiles are of different devices: /device:TPU:2 before, /device:TPU:8 now
where the time goes in v4:
time: 123 us; the launch traced here: 122 us
  Pallas kernels  122 us (99%)
    pallas_call x1, Pallas kernels, per_device(): pl.pallas_call(kernel, out_shape=shapes, in_specs=[vm, hbm, hbm, hbm], ou...  119 us
    pallas_call x1, Pallas kernels, per_device(): pl.pallas_call(finish, out_shape=shapes, in_specs=[vm] * 4, out_specs=(vm...  3 us

profile of v4, /device:TPU:8, one launch (start us, length us, event | category | flops | bytes accessed | tf_op | source)
XLA Modules:
  0.0 122.3 jit_solution(14664136842302815469)
XLA Ops:
  0.6 118.7 %shard_map.75 = (bf16[128,896]{1,0:T(8,128)(2,1)}, bf16[4,8192]{1,0:T(4,128)(2,1)}, bf16[512,896]{1,0:T(8,128)(2,1)}, bf16[512,896]{1,0:T(8,128)(2,1)}) custom-call(bf16[4,8192]{1,0:T(4,128)(2,1)} %tok_ref.1, bf16[512,896]{1,0:T(8,128)(2,1)} %gw_ref.1, bf16[512,896]{1,0:T(8,128)(2,1)} %uw_ref.1, bf16[128,896]{1,0:T(8,128)(2,1)} %hg_ref.1), custom_call_target="tpu_custom_call" | custom-call | flops 11299999744 | bytes 6000000 | tf_op jit(solution)/shard_map/pallas_call | solution.py:495
  119.3 3.0 %shard_map.76 = (bf16[128,896]{1,0:T(8,128)(2,1)}, bf16[4,8192]{1,0:T(4,128)(2,1)}, bf16[512,896]{1,0:T(8,128)(2,1)}, bf16[512,896]{1,0:T(8,128)(2,1)}) custom-call(bf16[128,896]{1,0:T(8,128)(2,1)} %get-tuple-element.8.refs_0_, bf16[4,8192]{1,0:T(4,128)(2,1)} %get-tuple-element.9.refs_1_, bf16[512,896]{1,0:T(8,128)(2,1)} %get-tuple-element.10.refs_2_, ...), custom_call_target="tpu_custom_call" | custom-call | tf_op jit(solution)/shard_map/pallas_call | solution.py:506
